TPU v7x, 32 devices: a whole 2x2x4 slice. The times are simulated.
32 devices in a mesh: batch: 8 (over y, x, core), blk: 4 (over z).
Axes of the slice: x: 2, y: 2, z: 4, core: 2. Of those that a mesh axis runs over, the one named last changes fastest.
Arguments:
- tokens: bfloat16 [32, 640, 768], P('batch', 'blk'), may hold values from -6 to 6
- resolution: int32 [32], P('batch'), may hold values from 0 to 1, as said below
- positions: int32 [32, 640], P('batch'), may hold values from 0 to 575, as said below
- ln1_gain: bfloat16 [768], replicated, may hold values from 0.5 to 1.5
- ln1_bias: bfloat16 [768], replicated, may hold values from -1.75 to 1.75
- w_qkv: bfloat16 [768, 2304], replicated, may hold values from -0.21875 to 0.21875
- q_bias: bfloat16 [768], replicated, may hold values from -3 to 3
- v_bias: bfloat16 [768], replicated, may hold values from -0.625 to 0.625
- w_proj: bfloat16 [768, 768], replicated, may hold values from -1.75 to 1.75
- proj_bias: bfloat16 [768], replicated, may hold values from -1.75 to 1.75
- gamma1: bfloat16 [768], replicated, may hold values from 0.5 to 2
- ln2_gain: bfloat16 [768], replicated, may hold values from 0.5 to 1.5
- ln2_bias: bfloat16 [768], replicated, may hold values from -1.75 to 1.75
- w_fc1: bfloat16 [768, 3072], replicated, may hold values from -0.21875 to 0.21875
- fc1_bias: bfloat16 [3072], replicated, may hold values from -3 to 3
- w_fc2: bfloat16 [3072, 768], replicated, may hold values from -0.109375 to 0.109375
- fc2_bias: bfloat16 [768], replicated, may hold values from -1.75 to 1.75
- gamma2: bfloat16 [768], replicated, may hold values from 0.5 to 2
- rel_low: bfloat16 [732, 12], replicated, may hold values from -4 to 4
- rel_high: bfloat16 [2212, 12], replicated, may hold values from -4 to 4
- grad_out: bfloat16 [32, 640, 768], P('batch', 'blk'), may hold values from -6 to 6
Outputs:
- output: bfloat16 [32, 640, 768], P('batch', 'blk')
- grad_tokens: bfloat16 [32, 640, 768], P('batch', 'blk')
- grad_ln1_gain: float32 [768], replicated
- grad_ln1_bias: float32 [768], replicated
- grad_w_qkv: float32 [768, 2304], P(('batch', 'blk'))
- grad_q_bias: float32 [768], replicated
- grad_v_bias: float32 [768], replicated
- grad_w_proj: float32 [768, 768], P(('batch', 'blk'))
- grad_proj_bias: float32 [768], replicated
- grad_gamma1: float32 [768], replicated
- grad_ln2_gain: float32 [768], replicated
- grad_ln2_bias: float32 [768], replicated
- grad_w_fc1: float32 [768, 3072], P(('batch', 'blk'))
- grad_fc1_bias: float32 [3072], replicated
- grad_w_fc2: float32 [3072, 768], P(('batch', 'blk'))
- grad_fc2_bias: float32 [768], replicated
- grad_gamma2: float32 [768], replicated
- grad_rel_low: float32 [732, 12], replicated
- grad_rel_high: float32 [2212, 12], replicated
Inputs may be any that keep to these rules, and one draw needn't show every extreme that they name: Among each 4 consecutive images (those of one index of batch) at least one has resolution 1. `positions`: for an image of grid side G, entries 1 to G * G hold every cell 0 to G * G - 1 once (cell = row * G + column); all other entries are 0.
All inputs are finite; a program needn't handle non-finite values.
Results may differ from a plain program's by a relative error of at most 0.015.
Values may be sent and summed in bfloat16 or wider, within the bound.
A program may use at most 384 MiB of HBM per device.

v0:
```python
import functools

import jax
import jax.numpy as jnp
import numpy as np
from jax import lax
from jax.experimental import pallas as pl
from jax.experimental.pallas import tpu as pltpu
from jax.sharding import PartitionSpec as P

G_LOW = 14
G_HIGH = 24
SIDE_LOW = 2 * G_LOW - 1
SIDE = 2 * G_HIGH - 1
CELLS = G_HIGH * G_HIGH
SPAN = 1152
F32 = jnp.float32
BF16 = jnp.bfloat16


def normalize(values):
    center = values - jnp.mean(values, axis=-1, keepdims=True)
    factor = lax.rsqrt(jnp.mean(center * center, axis=-1, keepdims=True) + 1e-06)
    return center * factor, factor


def norm_back(grad, normed, factor, gain):
    scaled = grad * gain
    return factor * (
        scaled
        - jnp.mean(scaled, axis=-1, keepdims=True)
        - normed * jnp.mean(scaled * normed, axis=-1, keepdims=True)
    )


def matmul(left, right):
    return jnp.dot(left, right, preferred_element_type=F32)


def matmul_t(left, right):
    return lax.dot_general(left, right, (((1,), (1,)), ((), ())), preferred_element_type=F32)


def t_matmul(left, right):
    return lax.dot_general(left, right, (((0,), (0,)), ((), ())), preferred_element_type=F32)


def slot_tables(seq):
    tokens = np.arange(seq)
    tables = []
    for grid in (G_LOW, G_HIGH):
        cells = np.arange(CELLS)
        used = (cells // G_HIGH < grid) & (cells % G_HIGH < grid)
        free = np.concatenate([cells[~used], np.arange(CELLS + 1, seq)])
        slot = np.full(seq, CELLS)
        slot[1 + grid * grid :] = free
        patch = np.concatenate([used, np.zeros(seq - CELLS, bool)])
        key = patch.copy()
        key[CELLS] = True
        tables.append((slot, (tokens >= 1) & (tokens < 1 + grid * grid), patch, key))
    return [np.stack(parts) for parts in zip(*tables)]


def lane_tables():
    lanes = np.arange(SPAN)
    shift = G_HIGH - 1 - lanes % G_HIGH
    bits = (shift[None, :] >> np.arange(8)[:, None]) & 1
    return bits.astype(np.int32)


def spread_of(rows, first):
    row = (lax.broadcasted_iota(jnp.int32, (rows, SPAN), 0) - first) * G_HIGH
    lane = lax.broadcasted_iota(jnp.int32, (rows, SPAN), 1) - row
    inside = (lane >= 0) & (lane < G_HIGH) & (row >= 0) & (row < SIDE * G_HIGH)
    return jnp.where(inside, 1.0, 0.0).astype(BF16)


def slide(values, bits, down):
    for k in range(5):
        amount = 1 << k if down else 48 - (1 << k)
        values = jnp.where(bits[k : k + 1, :] > 0, pltpu.roll(values, amount, 0), values)
    return values


VMEM_LIMIT = 62 << 20


def whole(shape):
    return pl.BlockSpec(shape, lambda h: (0,) * len(shape))


def once(shape):
    return pl.BlockSpec(shape, lambda h: (0,) * len(shape), pipeline_mode=pl.Buffered(1))


ANY = pl.BlockSpec(memory_space=pl.ANY)
SMEM = pl.BlockSpec(memory_space=pltpu.SMEM)


def flat_row(ref):
    return ref[...].astype(F32).reshape(1, ref.shape[0])


def front_kernel(
    count, resolution, cells, low_t, high_t, bits, slot_of, is_patch, patches, masks,
    ln1_gain, ln1_bias, q_bias, v_bias, w_qkv, tokens, grad_out,
    to_slot, inputs, qkv, probs, mixed, raw_up, bias, raw, landed, inner_low, inner_high, wide, full, spread, *refs,
):
    step = pl.program_id(0)
    me = lax.axis_index("blk")
    high = resolution[me] == 1
    seq = full.shape[0]
    heads = low_t.shape[0]
    width = inputs.shape[1]
    size = len(Exchange(count).scratch())
    move = Exchange(count).bind(tokens, raw, refs[:size])
    move_up = Exchange(count).bind(grad_out, landed, refs[size:])

    @pl.when(step == 0)
    def _():
        greet(move.partners())
        move.start()
        here = cells[pl.ds(me, 1), :]
        grid = jnp.where(high, G_HIGH, G_LOW)
        row = jnp.zeros_like(here)
        for k in range(1, G_HIGH):
            row += (here >= k * grid).astype(jnp.int32)
        at = row * G_HIGH + here - row * grid
        patch = jnp.where(high, is_patch[1:2, :], is_patch[0:1, :])
        other = jnp.where(high, slot_of[1:2, :], slot_of[0:1, :])
        slot = jnp.where(patch > 0, at, other)
        spots = lax.broadcasted_iota(jnp.int32, (seq, seq), 0)
        to_slot[...] = jnp.where(spots == slot, 1.0, 0.0).astype(BF16)
        spread[...] = spread_of(48, 0)
        inner_low[...] = jnp.zeros_like(inner_low)
        inner_high[...] = jnp.zeros_like(inner_high)
        low_f, high_f = low_t[...].astype(F32), high_t[...].astype(F32)
        pad = G_HIGH - G_LOW
        for j in range(SIDE):
            r = SIDE - 1 - j
            inner_high[j * 16 : j * 16 + heads, 0:SIDE] = high_f[:, r * SIDE : (r + 1) * SIDE]
            r -= pad
            if 0 <= r < SIDE_LOW:
                inner_low[j * 16 : j * 16 + heads, pad : pad + SIDE_LOW] = low_f[
                    :, r * SIDE_LOW : (r + 1) * SIDE_LOW
                ]

    @pl.when(step < heads)
    def _():
        rows = pl.ds(step, 48, stride=16)
        table = jnp.where(high, inner_high[rows, :], inner_low[rows, :]).astype(BF16)
        wide[...] = slide(t_matmul(table, spread[...])[0:48], bits, False)[0:G_HIGH]
        for r in range(G_HIGH):
            at = (G_HIGH - 1 - r) * G_HIGH
            full[r * G_HIGH : (r + 1) * G_HIGH, 0:CELLS] = wide[:, at : at + CELLS]
        column = lax.broadcasted_iota(jnp.int32, (1, seq), 1)
        ends = [t[:, t.shape[1] - 3 : t.shape[1]].astype(F32) for t in (low_t, high_t)]
        special = jnp.where(high, ends[1], ends[0])
        here = lax.broadcasted_iota(jnp.int32, special.shape, 0) == step
        special = jnp.sum(jnp.where(here, special, 0.0), axis=0, keepdims=True)
        inner_row = jnp.where(column < CELLS, special[:, 0:1], special[:, 2:3])
        values = jnp.where(column < CELLS, full[...], special[:, 1:2])
        patch = jnp.where(high, patches[:, 1:2], patches[:, 0:1])
        mask = jnp.where(high, masks[1:2, :], masks[0:1, :])
        values = jnp.where(patch > 0.0, values, inner_row)
        bias[step] = (values + mask).astype(BF16)

    @pl.when(step == heads)
    def _():
        move.finish()
        move_up.start()
        value = matmul(to_slot[...], raw[...].reshape(seq, width))
        inputs[...] = value
        hidden = (normalize(value)[0] * flat_row(ln1_gain) + flat_row(ln1_bias)).astype(BF16)
        shifts = [flat_row(q_bias), 0.0, flat_row(v_bias)]
        for n in range(3):
            part = slice(n * width, (n + 1) * width)
            qkv[:, part] = (matmul(hidden, w_qkv[:, part]) + shifts[n]).astype(BF16)

    @pl.when(step >= heads)
    def _():
        pair = step - heads
        query, keys, values = [
            qkv[:, pl.ds(pl.multiple_of(n * width + pair * 128, 128), 128)] for n in range(3)
        ]
        for h in range(2):
            at = slice(h * 64, h * 64 + 64)
            scores = matmul_t(query[:, at] * 0.125, keys[:, at]) + bias[2 * pair + h].astype(F32)
            expo = jnp.exp(scores - jnp.max(scores, axis=-1, keepdims=True))
            low = (expo * (1.0 / jnp.sum(expo, axis=-1, keepdims=True))).astype(BF16)
            probs[h] = low
            mixed[:, at] = matmul(low, values[:, at]).astype(BF16)

    @pl.when(step == pl.num_programs(0) - 1)
    def _():
        move_up.finish()
        raw_up[...] = landed[...]


def front(resolution, cells, rel_low, rel_high, bits, patches, vectors, w_qkv, tokens, grad_out, count):
    heads = rel_low.shape[1]
    seq = cells.shape[1]
    width = w_qkv.shape[0]
    slot_np, token_np, _, key_np = slot_tables(seq)
    slot_of = jnp.asarray(slot_np, jnp.int32)
    is_patch = jnp.asarray(token_np, jnp.int32)
    masks = jnp.asarray(np.where(key_np, 0.0, -1e30), F32)
    operands = (rel_low.T, rel_high.T, bits, slot_of, is_patch, patches, masks) + vectors + (w_qkv,)
    late = lambda i: jnp.maximum(i - heads, 0)
    return pl.pallas_call(
        functools.partial(front_kernel, count),
        grid=(heads + heads // 2,),
        out_shape=(
            jax.ShapeDtypeStruct((seq, seq), BF16),
            jax.ShapeDtypeStruct((seq, width), F32),
            jax.ShapeDtypeStruct((seq, 3 * width), BF16),
            jax.ShapeDtypeStruct((heads, seq, seq), BF16),
            jax.ShapeDtypeStruct((seq, width), BF16),
            jax.ShapeDtypeStruct(grad_out.shape, BF16),
        ),
        in_specs=[SMEM, whole(cells.shape)] + [whole(o.shape) for o in operands] + [ANY, ANY],
        out_specs=(
            whole((seq, seq)),
            whole((seq, width)),
            whole((seq, 3 * width)),
            pl.BlockSpec((2, seq, seq), lambda i: (late(i), 0, 0)),
            pl.BlockSpec((seq, 128), lambda i: (0, late(i))),
            once(grad_out.shape),
        ),
        scratch_shapes=[
            pltpu.VMEM((heads, seq, seq), BF16),
            pltpu.VMEM(tokens.shape, BF16),
            pltpu.VMEM(grad_out.shape, BF16),
            pltpu.VMEM((48 * 16, 128), F32),
            pltpu.VMEM((48 * 16, 128), F32),
            pltpu.VMEM((G_HIGH, SPAN), F32),
            pltpu.VMEM((seq, seq), F32),
            pltpu.VMEM((48, SPAN), BF16),
        ]
        + Exchange(count).scratch()
        + Exchange(count).scratch(),
        compiler_params=pltpu.CompilerParams(
            collective_id=0, has_side_effects=True, vmem_limit_bytes=VMEM_LIMIT
        ),
        name="front",
    )(resolution, cells, *operands, tokens, grad_out)


def head_grads(query, keys, values, weights, up, patch, spread, bits, score, wide, lanes):
    ups = matmul_t(up, values)
    weight = weights.astype(F32)
    product = weight * ups
    ds = product - weight * jnp.sum(product, axis=-1, keepdims=True)
    ds_low = ds.astype(BF16)
    d_query = (matmul(ds_low, keys) * 0.125).astype(BF16)
    d_key = t_matmul(ds_low, query * 0.125).astype(BF16)
    d_value = t_matmul(weights, up).astype(BF16)
    total = jnp.sum(ds, axis=0, keepdims=True)
    ds = ds * patch
    score[...] = ds
    inside = jnp.sum(ds, axis=0, keepdims=True)
    wide[...] = jnp.zeros_like(wide)
    for r in range(G_HIGH):
        off = (G_HIGH - 1 - r) * G_HIGH
        wide[:, off : off + CELLS] += score[r * G_HIGH : (r + 1) * G_HIGH, 0:CELLS]
    flat = slide(jnp.concatenate([wide[...], jnp.zeros_like(wide)], axis=0), bits, True)
    first = flat.astype(BF16)
    rest = flat - first.astype(F32)
    second = rest.astype(BF16)
    third = (rest - second.astype(F32)).astype(BF16)
    table = matmul_t(first, spread) + matmul_t(second, spread) + matmul_t(third, spread)
    column = lax.broadcasted_iota(jnp.int32, total.shape, 1)
    lane = lax.broadcasted_iota(jnp.int32, (1, 128), 1)
    outside = total - inside
    edge = jnp.zeros((1, 128), F32)
    for i, value in enumerate((
        jnp.where(column < CELLS, outside, 0.0),
        jnp.where(column == CELLS, inside, 0.0),
        jnp.where(column == CELLS, outside, 0.0),
    )):
        edge += jnp.where(lane == lanes + i, jnp.sum(value, axis=1, keepdims=True), 0.0)
    return d_query, d_key, d_value, table, edge


def by_lanes(row):
    return jnp.concatenate([row[:, i : i + 128] for i in range(0, row.shape[1], 128)], axis=0)


FC1_SLOTS = ((0, 2, 6, 10, 13, 20, 26), (0, 3, 8, 11, 13, 20, 26), (1, 3, 9, 12, 14, 20, 26))
PROJ_SLOTS = ((8, 10, 13, 16, 21, 22, 26),)
QKV_SLOTS = (
    (8, 10, 13, 16, 21, 22, 26),
    (9, 11, 16, 17, 21, 22, 26),
    (12, 13, 17, 18, 21, 22, 26),
)
FC2_SLOTS = ((0, 4, 7, 18, 26), (0, 5, 8, 18, 26))
EARLY_SLOTS = (0, 1, 3, 5, 7, 9)
TABLE_SLOTS = ((8, 9, 11, 16, 17, 18), (12, 13, 16, 17, 18, 19))
LATE_SLOTS = (15, 15, 16, 17, 18, 19)
TABLE_PAIRS = 4


def tail_kernel(setup, *refs):
    count, groups, grads = setup
    direct = grads > 0
    fc1_pairs, proj_pairs, fc2_second, qkv_groups = groups
    refs = list(refs)
    take = lambda n: [refs.pop(0) for _ in range(n)]
    resolution, query, keys, values, probs, upstream, patches, bits, ln1_gain, ln1_bias = take(10)
    sources = take(4)
    partials = take(grads)
    early, *p_fc2 = take(1 + len(fc2_second)) if direct else [None]
    moved, g_qkv = take(2)
    g_fc1, g_proj, g_fc2, early_sum = take(4) if direct else [None] * 4
    late_sum, table_sum = take(2)
    score, wide, d_qkv, hidden, table_a, table_b, tokens, landed, late, spread = take(10)
    loaded = take(4)
    load_sems = take(1)[0]
    move = Exchange(count)
    move.bind(tokens, landed, take(len(move.scratch())))
    step = pl.program_id(0)
    steps = pl.num_programs(0) - 1
    seq, width = loaded[0].shape
    first_rows = table_a.shape[1]
    slots = [[] for _ in range(28)]

    def run(slot):
        for tick in slots[slot]:
            tick()

    if direct:
        grad = take(1)[0]
        scratch_of = lambda part: take(len(part.scratch()))

        def plan(bound, own, numbers=range(7)):
            for number, slot in zip(numbers, own):
                slots[slot].append(functools.partial(run_stage, bound, number))

        small = VectorSum(early.shape[1:])
        plan([small.bind(early, early_sum, scratch_of(small))], EARLY_SLOTS)
        for ref, at, own in zip((table_a, table_b), (0, first_rows), TABLE_SLOTS):
            part = VectorSum(ref.shape[1:], True)
            plan([part.bind(ref, table_sum, scratch_of(part), at)], own)
        part = VectorSum(late.shape, split=False)
        plan([part.bind(late, late_sum, scratch_of(part))], LATE_SLOTS)
        for pair, own, source in zip(fc2_second, FC2_SLOTS, p_fc2):
            bound = [part.bind(source.at[f], g_fc2, scratch_of(part)) for f, part in enumerate(pair)]
            plan(bound, own, (2, 3, 4, 5, 6))
        for k, (pair, spots) in enumerate(zip(fc1_pairs, FC1_SLOTS)):
            plan([part.bind(partials[0].at[2 * k + f], g_fc1, scratch_of(part), 0) for f, part in enumerate(pair)], spots)
        for pair, spots in zip(proj_pairs, PROJ_SLOTS):
            plan([part.bind(partials[1], g_proj, scratch_of(part)) for part in pair], spots)
        for group, spots in zip(qkv_groups, QKV_SLOTS):
            plan([part.bind(grad, g_qkv, scratch_of(part)) for part in group], spots)

    loads = [
        pltpu.make_async_copy(source, target, load_sems.at[i])
        for i, (source, target) in enumerate(zip(sources, loaded))
    ]
    inputs, d_resid, to_slot, w_qkv = loaded

    @pl.when(step == 0)
    def _():
        greet(sum_partners() if direct else move.partners())
        for load in loads:
            load.start()
        for h in range(2):
            spread[h] = spread_of(128, 64 * h)

    high = resolution[lax.axis_index("blk")] == 1

    @pl.when(step < steps)
    def _():
        patch = jnp.where(high, patches[:, 1:2], patches[:, 0:1])
        total = jnp.zeros((48, 128), F32)
        edge = jnp.zeros((1, 128), F32)
        parts3 = [[], [], []]
        for h in range(2):
            for k in range(6):
                if slots[2 * k + h]:
                    pl.when(step == k)(functools.partial(run, 2 * k + h))

            at = slice(h * 64, h * 64 + 64)
            *heads3, part, ends = head_grads(
                query[:, at], keys[:, at], values[:, at], probs[h], upstream[:, at],
                patch, spread[h], bits, score, wide, h * 64,
            )
            total += part
            edge += ends
            for n in range(3):
                parts3[n].append(heads3[n])
        for n in range(3):
            at = pl.ds(pl.multiple_of(n * width + step * 128, 128), 128)
            d_qkv[:, at] = jnp.concatenate(parts3[n], axis=1)
        row = lax.broadcasted_iota(jnp.int32, (48, 128), 0)
        total = jnp.where(row == 47, edge, total)
        for k in range(6):

            @pl.when(step == k)
            def _(k=k):
                ref, at = (table_a, k) if k < TABLE_PAIRS else (table_b, k - TABLE_PAIRS)
                ref[0, at * 48 : at * 48 + 48, :] = jnp.where(high, 0.0, total)
                ref[1, at * 48 : at * 48 + 48, :] = jnp.where(high, total, 0.0)

    @pl.when(step == 1)
    def _():
        loads[0].wait()
        hidden[...] = (normalize(inputs[...])[0] * flat_row(ln1_gain) + flat_row(ln1_bias)).astype(BF16)

    for k in range(3):

        @pl.when(step == 2 * k + 1)
        def _(k=k):
            for n in range(3):
                at = slice(n * width + k * 256, n * width + k * 256 + 256)
                partial = t_matmul(hidden[...], d_qkv[:, at]).astype(BF16)
                if direct:
                    grad[:, :, :, :, at] = partial.reshape(2, 2, 2, width // 8, 256)
                else:
                    g_qkv[:, at] = partial

    @pl.when(step == steps)
    def _():
        run(12)
        for load in loads[1:]:
            load.wait()
        gain = flat_row(ln1_gain)
        def enter(rows, totals):
            d_gain, d_shift = totals
            back = matmul_t(d_qkv[rows, :], w_qkv[...])
            value, scale = normalize(inputs[rows, :])
            hidden[rows, :] = (d_resid[rows, :] + norm_back(back, value, scale, gain)).astype(BF16)
            return d_gain + row_sum(back * value), d_shift + row_sum(back)

        d_gain, d_shift = row_blocks(seq, seq // 2, enter, (jnp.zeros((1, width), F32),) * 2)
        run(13)
        run(14)
        ordered = t_matmul(to_slot[...], hidden[...]).astype(BF16)
        tokens[...] = ordered.reshape(tokens.shape)
        sums4 = [d_gain, d_shift] + [
            row_sum(d_qkv[:, n * width : (n + 1) * width].astype(F32)) for n in (0, 2)
        ]
        late[...] = jnp.concatenate([by_lanes(v) for v in sums4], axis=0)
        run(15)
        move.start()
        if direct:
            for slot in range(16, 28):
                run(slot)
        else:
            late_sum[...] = late[...]
            table_sum[:, 0:first_rows] = table_a[...]
            table_sum[:, first_rows:] = table_b[...]
        move.finish()
        moved[...] = landed[...]


def tail(resolution, qkv, probs, upstream, patches, bits, vectors, inputs, d_resid, to_slot, w_qkv, partials, p_fc2, early, count, direct):
    seq, width = inputs.shape
    steps = width // 128
    clip = lambda h: jnp.minimum(h, steps - 1)
    column = lambda part: pl.BlockSpec((seq, 128), lambda h: (0, part * steps + clip(h)))
    blocks = jax.ShapeDtypeStruct((count, seq // count, width), BF16)
    late, table = (24, 128), (2, 48 * steps, 128)
    tables = [(2, 48 * TABLE_PAIRS, 128), (2, 48 * (steps - TABLE_PAIRS), 128)]
    groups, views, more, outs = ((), (), (), ()), [], [], []
    g_qkv = jax.ShapeDtypeStruct((width, 3 * width), BF16)
    if direct:
        views = [g.reshape(*g.shape[:-2], 2, 2, 2, g.shape[-2] // 8, g.shape[-1]) for g in partials]
        more = [early, *p_fc2]
        chunks, _, chunk = partials[0].shape
        hidden = chunks * chunk
        share = lambda columns, rows=width: jax.ShapeDtypeStruct((rows // 32, columns), F32)
        outs = [share(hidden), share(width), share(width, hidden), jax.ShapeDtypeStruct(early.shape, F32)]
        g_qkv = share(3 * width)
        fc1_pairs = [
            [WeightSum(width // 8, (2 * k + f) * chunk, chunk, f == 1) for f in (0, 1)] for k in range(chunks // 2)
        ]
        proj_pairs = [[WeightSum(width // 8, 0, 256, False), WeightSum(width // 8, 256, 512, True)]]
        fc2_second = fc2_pairs(hidden, "second")
        qkv_groups = [
            [WeightSum(width // 8, n * width + k * 256, 256, (n + k) % 2 == 1, True) for n in range(3)]
            for k in range(3)
        ]
        groups = (fc1_pairs, proj_pairs, fc2_second, qkv_groups)
    outs = list(outs) + [jax.ShapeDtypeStruct(late, F32), jax.ShapeDtypeStruct(table, F32)]
    held = (inputs, d_resid, to_slot, w_qkv)
    scratch = [
        pltpu.VMEM((seq, seq), F32),
        pltpu.VMEM((G_HIGH, SPAN), F32),
        pltpu.VMEM((seq, 3 * width), BF16),
        pltpu.VMEM((seq, width), BF16),
        pltpu.VMEM(tables[0], F32),
        pltpu.VMEM(tables[1], F32),
        pltpu.VMEM(blocks.shape, BF16),
        pltpu.VMEM(blocks.shape, BF16),
        pltpu.VMEM(late, F32),
        pltpu.VMEM((2, 128, SPAN), BF16),
    ]
    scratch += [pltpu.VMEM(o.shape, o.dtype) for o in held] + [pltpu.SemaphoreType.DMA((4,))]
    scratch += Exchange(count).scratch()
    if direct:
        scratch.append(pltpu.VMEM((2, 2, 2, width // 8, 3 * width), BF16))
        parts = [VectorSum(early.shape[1:])] + [VectorSum(t[1:], True) for t in tables] + [VectorSum(late, split=False)]
        parts += [part for pair in fc2_second + fc1_pairs + proj_pairs + qkv_groups for part in pair]
        scratch += [s for part in parts for s in part.scratch()]
    return pl.pallas_call(
        functools.partial(tail_kernel, (count, groups, len(views))),
        grid=(steps + 1,),
        out_shape=[blocks, g_qkv] + outs,
        in_specs=[
            SMEM,
            column(0),
            column(1),
            column(2),
            pl.BlockSpec((2, seq, seq), lambda h: (clip(h), 0, 0)),
            column(0),
            whole(patches.shape),
            whole(bits.shape),
        ]
        + [whole(v.shape) for v in vectors]
        + [ANY] * (4 + len(views))
        + [whole(v.shape) for v in more],
        out_specs=[once(blocks.shape), whole(g_qkv.shape)] + [whole(o.shape) for o in outs],
        scratch_shapes=scratch,
        compiler_params=pltpu.CompilerParams(
            collective_id=2, has_side_effects=True, vmem_limit_bytes=VMEM_LIMIT
        ),
        name="tail",
    )(resolution, qkv, qkv, qkv, probs, upstream, patches, bits, *vectors, *held, *views, *more)


MESH = pl.DeviceIdType.MESH


def place():
    b, z = lax.axis_index("batch"), lax.axis_index("blk")
    return b, z, lax.rem(b, 2), lax.rem(b // 2, 2), b // 4


def greet(partners):
    barrier = pltpu.get_barrier_semaphore()
    for partner in partners:
        pl.semaphore_signal(barrier, inc=1, device_id=partner, device_id_type=MESH)
    pl.semaphore_wait(barrier, len(partners))


def sum_partners():
    b, z, c, x, y = place()
    near = [(b + 1 - 2 * c, z), (b + 2 - 4 * x, z), (b + 4 - 8 * y, z)]
    return near + [(b, lax.rem(z + s, 4)) for s in (1, 2, 3)]


class Exchange:
    def __init__(self, count):
        self.count = count

    def scratch(self):
        sems = pltpu.SemaphoreType.DMA((self.count - 1,))
        return [sems, sems, pltpu.SemaphoreType.DMA]

    def bind(self, source, target, refs):
        self.source, self.target = source, target
        self.sent, self.come, self.own = refs
        return self

    def partners(self):
        b, z = lax.axis_index("batch"), lax.axis_index("blk")
        return [(b, lax.rem(z + s, self.count)) for s in range(1, self.count)]

    def local(self):
        z = lax.axis_index("blk")
        return pltpu.make_async_copy(self.source.at[z], self.target.at[z], self.own)

    def copy(self, i):
        device = self.partners()[i]
        return pltpu.make_async_remote_copy(
            src_ref=self.source.at[device[1]],
            dst_ref=self.target.at[lax.axis_index("blk")],
            send_sem=self.sent.at[i],
            recv_sem=self.come.at[i],
            device_id=device,
            device_id_type=MESH,
        )

    def start(self):
        for i in range(self.count - 1):
            self.copy(i).start()
        self.local().start()

    def finish(self):
        self.local().wait()
        for i in range(self.count - 1):
            self.copy(i).wait_recv()
        for i in range(self.count - 1):
            self.copy(i).wait_send()


class VectorSum:
    STAGES = 6

    def __init__(self, size, low=False, split=True):
        self.size, self.dtype, self.split = tuple(size), BF16 if low else F32, split

    def scratch(self):
        part = pltpu.VMEM(self.size, F32)
        sems = pltpu.SemaphoreType.DMA((7,))
        return [part] * 7 + [pltpu.VMEM((4,) + self.size, self.dtype), sems, sems]

    def bind(self, source, target, refs, at=0):
        self.source, self.target, self.at = source, target, at
        self.got0, self.sum1, self.got1, self.sum2, self.got2, self.mine, self.other, self.all = refs[:8]
        self.sent, self.come = refs[8:]
        return self

    def copy(self, i):
        b, z, c, x, y = place()
        near = sum_partners()
        source, target, device = (
            (self.source.at[1 - c] if self.split else None, self.got0, near[0]),
            (self.all.at[z], self.all.at[z], near[3]),
            (self.all.at[z], self.all.at[z], near[4]),
            (self.all.at[z], self.all.at[z], near[5]),
            (self.sum1, self.got1, near[1]),
            (self.sum2, self.got2, near[2]),
            (self.mine, self.other, near[0]),
        )[i]
        return pltpu.make_async_remote_copy(
            src_ref=source,
            dst_ref=target,
            send_sem=self.sent.at[i],
            recv_sem=self.come.at[i],
            device_id=device,
            device_id_type=MESH,
        )

    def stage(self, number):
        b, z, c, x, y = place()
        if number == 0:
            if self.split:
                self.copy(0).start()
        elif number == 1:
            if self.split:
                self.copy(0).wait_recv()
                self.all[z] = (self.source[c] + self.got0[...]).astype(self.dtype)
            else:
                self.all[z] = self.source[...].astype(self.dtype)
            for i in (1, 2, 3):
                self.copy(i).start()
        elif number == 2:
            for i in (1, 2, 3):
                self.copy(i).wait_recv()
            value = [self.all[k].astype(F32) for k in range(4)]
            self.sum1[...] = value[0] + value[1] + value[2] + value[3]
            self.copy(4).start()
        elif number == 3:
            self.copy(4).wait_recv()
            self.sum2[...] = self.sum1[...] + self.got1[...]
            self.copy(5).start()
        elif number == 4:
            self.copy(5).wait_recv()
            self.mine[...] = self.sum2[...] + self.got2[...]
            self.copy(6).start()
        else:
            self.copy(6).wait_recv()
            if self.split:
                rows = slice(self.at, self.at + self.size[0])
                self.target[c, rows] = self.mine[...]
                self.target[1 - c, rows] = self.other[...]
            else:
                self.target[...] = self.mine[...] + self.other[...]
            for i in range(0 if self.split else 1, 7):
                self.copy(i).wait_send()


def in_steps(rows, width, body):
    step = rows
    while step * width > 49152 and step % 32 == 0:
        step //= 2
    if step == rows:
        body(pl.ds(0, rows))
    else:

        def one(i, carry):
            body(pl.ds(pl.multiple_of(i * step, step), step))
            return carry

        lax.fori_loop(0, rows // step, one, 0)


class WeightSum:
    COPIES = 5

    def __init__(self, rows, at, width, flip, resident=False, half=""):
        self.rows, self.at, self.width, self.flip, self.resident = rows, at, width, flip, resident
        self.half = half
        self.fold = 2 if (rows // 4) % 16 else 1

    def strip(self):
        return (self.rows // 4 * self.fold, self.width // self.fold)

    def scratch(self):
        r, w = self.rows, self.width
        strip = self.strip()
        refs = [pltpu.SemaphoreType.DMA((self.COPIES,))] * 2
        if self.half != "first":
            refs += [pltpu.VMEM((2, 2) + strip, BF16), pltpu.VMEM((2,) + strip, BF16), pltpu.VMEM(strip, BF16)]
            refs += [pltpu.VMEM((r, w), BF16)]
        if self.half != "second":
            refs += [pltpu.VMEM((2, 2, r, w), BF16), pltpu.VMEM((2, r, w), BF16)]
            if not self.resident:
                refs += [pltpu.VMEM((2, 2, r, w), BF16), pltpu.SemaphoreType.DMA]
        return refs

    def bind(self, grad, out, refs, at=None):
        self.grad, self.out = grad, out
        self.source_at = self.at if at is None else at
        refs = list(refs)
        take = lambda n: [refs.pop(0) for _ in range(n)]
        self.sent, self.come = take(2)
        if self.half != "first":
            self.mine, self.got3, self.got4, self.got2 = take(4)
        if self.half != "second":
            self.got0, self.got1 = take(2)
            if not self.resident:
                self.kept, self.own = take(2)
        return self

    def columns(self):
        return pl.ds(self.source_at, self.width)

    def keep(self, i, j):
        if self.half == "second":
            return self.grad.at[j if self.flip else i]
        if self.resident:
            return self.grad.at[i, j, place()[2], :, self.columns()]
        return self.kept.at[i, j]

    def local(self):
        c = place()[2]
        return pltpu.make_async_copy(self.grad.at[:, :, c, :, self.columns()], self.kept, self.own)

    def copy(self, i):
        b, z, c, x, y = place()
        to = sum_partners()
        every = slice(None)
        if i == 0:
            source, target, device = self.grad.at[:, :, 1 - c, :, self.columns()], self.got0, to[0]
        elif i == 1:
            source = self.keep(1 - y, every) if self.flip else self.keep(every, 1 - x)
            target, device = self.got1, to[2 if self.flip else 1]
        elif i == 2:
            source = self.keep(y, 1 - x) if self.flip else self.keep(1 - y, x)
            target, device = self.got2, to[1 if self.flip else 2]
        elif i == 3:
            z0 = lax.rem(z, 2)
            source, target, device = self.mine.at[:, 1 - z0], self.got3, (b, z + 1 - 2 * z0)
        else:
            z0, z1 = lax.rem(z, 2), z // 2
            source, target, device = self.mine.at[1 - z1, z0], self.got4, (b, z + 2 - 4 * z1)
        return pltpu.make_async_remote_copy(
            src_ref=source,
            dst_ref=target,
            send_sem=self.sent.at[i],
            recv_sem=self.come.at[i],
            device_id=device,
            device_id_type=MESH,
        )

    def add(self, target, source):
        self.put(target, target, source)

    def put(self, target, first, second):
        def body(rows):
            target[rows, :] = first[rows, :] + second[rows, :]

        in_steps(self.rows, self.width, body)

    def stage(self, number):
        b, z, c, x, y = place()
        keep = self.keep
        if self.half != "second":
            got0, got1 = self.got0, self.got1
        if self.half == "second" and number == 2:
            self.copy(2).start()
            return
        if self.half == "first" and number == 2:
            self.copy(1).wait_recv()
            for k in range(2):
                self.put(self.out.at[k], keep(y, k) if self.flip else keep(k, x), got1.at[k])
            return
        if number == 0:
            if not self.resident:
                self.local().start()
            self.copy(0).start()
        elif number == 1:
            if not self.resident:
                self.local().wait()
            self.copy(0).wait_recv()
            spots = lambda k: [(k, 0), (k, 1)] if self.flip else [(0, k), (1, k)]
            mine = y if self.flip else x
            for i, j in spots(1 - mine):
                self.add(keep(i, j), got0.at[i, j])
            self.copy(1).start()
            for i, j in spots(mine):
                self.add(keep(i, j), got0.at[i, j])
        elif number == 2:
            self.copy(1).wait_recv()
            if self.flip:
                self.add(keep(y, 1 - x), got1.at[1 - x])
                self.copy(2).start()
                self.add(keep(y, x), got1.at[x])
            else:
                self.add(keep(1 - y, x), got1.at[1 - y])
                self.copy(2).start()
                self.add(keep(y, x), got1.at[y])
        elif number == 3:
            self.copy(2).wait_recv()
            r = self.rows // 4
            mine = keep(y, x)
            for k in range(4):
                rows = slice(k * r, k * r + r)
                value = mine[rows, :].astype(F32) + self.got2[rows, :].astype(F32)
                if self.fold == 2:
                    half = self.width // 2
                    value = jnp.concatenate([value[:, :half], value[:, half:]], axis=0)
                self.mine[k // 2, k % 2] = value.astype(BF16)
            self.copy(3).start()
        elif number == 4:
            self.copy(3).wait_recv()
            z0, z1 = lax.rem(z, 2), z // 2
            self.mine[1 - z1, z0] = self.mine[1 - z1, z0] + self.got3[1 - z1]
            self.copy(4).start()
        elif number == 5:
            self.copy(4).wait_recv()
            z0, z1 = lax.rem(z, 2), z // 2
            value = self.mine[z1, z0].astype(F32) + self.got3[z1].astype(F32) + self.got4[...].astype(F32)
            r, half = self.rows // 4, self.width // 2
            if self.fold == 2:
                self.out[:, self.at : self.at + half] = value[:r]
                self.out[:, self.at + half : self.at + self.width] = value[r:]
            else:
                self.out[:, self.at : self.at + self.width] = value
        else:
            for i in {"": range(5), "first": range(2), "second": range(2, 5)}[self.half]:
                self.copy(i).wait_send()


def run_stage(pair, number):
    for part in pair:
        part.stage(number)


def row_blocks(rows, size, body, carry):
    return lax.fori_loop(
        0, rows // size, lambda i, c: body(pl.ds(pl.multiple_of(i * size, size), size), c), carry
    )


def row_sum(values):
    return jnp.sum(values, axis=0, keepdims=True)


MLP_ROWS = 320
MLP_CHUNK = 512
FC2_SPANS = (512, 256)
MLP_SLOTS = (
    (0, 5, 20, 21),
    (3, 6, 21, 21),
)


def mlp_kernel(setup, *refs):
    count, direct, pairs = setup
    refs = list(refs)
    take = lambda n: [refs.pop(0) for _ in range(n)]
    inputs, mixed, raw_up, to_slot, w_proj, *vectors = take(11)
    b1, w1_all, w2_all = take(3)
    output, d_resid, d_mixed, p_proj, p_fc1, vector, *p_fc2 = take(6 + (len(pairs) or 1))
    hidden, d_branch, upstream, attn, resid, branch, d_hidden, act, slope, d_pre, d_bias, blocks_out, landed = take(13)
    held1, held2, load_sems = take(3)
    move = Exchange(count)
    move.bind(blocks_out, landed, take(len(move.scratch())))
    step = pl.program_id(0)
    seq, width = inputs.shape
    steps, _, chunk = held1.shape
    w1, w2 = held1.at[lax.rem(step, steps)], held2.at[lax.rem(step, steps)]
    proj_bias, gain1, gain2, shift2, fc2_bias, gain_out = [flat_row(v) for v in vectors]
    slots = [[] for _ in range(3 * steps + 4)]
    at_chunk = pl.ds(pl.multiple_of(lax.rem(step, steps) * chunk, chunk), chunk)
    grads = []

    def run(slot):
        for tick in slots[slot]:
            tick()

    def run_here(spot):
        for k in range(steps):
            if slots[3 * k + spot]:
                pl.when(step == steps + k)(functools.partial(run, 3 * k + spot))

    if direct:
        grads = take(len(pairs))
        for n, (grad, pair) in enumerate(zip(grads, pairs)):
            bound = [
                part.bind(grad, p_fc2[n].at[f], take(len(part.scratch())), at=f * part.width)
                for f, part in enumerate(pair)
            ]
            for number, slot in zip((0, 1, 2, 6), MLP_SLOTS[n]):
                slots[slot].append(functools.partial(run_stage, bound, number))

    def load(k):
        at = slice(k * chunk, (k + 1) * chunk)
        return [
            pltpu.make_async_copy(w1_all.at[:, at], held1.at[k], load_sems.at[2 * k]),
            pltpu.make_async_copy(w2_all.at[at, :], held2.at[k], load_sems.at[2 * k + 1]),
        ]

    @pl.when(step == 0)
    def _():
        for k in range(steps):
            for copy in load(k):
                copy.start()
        greet(sum_partners() if direct else move.partners())
        d_bias[...] = flat_row(b1)

        def enter(rows, carry):
            up = matmul(to_slot[rows, :], raw_up[...])
            upstream[rows, :] = up
            d_branch[rows, :] = (gain_out * up).astype(BF16)
            value = matmul(mixed[rows, :], w_proj[...]) + proj_bias
            attn[rows, :] = value
            value = inputs[rows, :] + gain1 * value
            resid[rows, :] = value
            hidden[rows, :] = (normalize(value)[0] * gain2 + shift2).astype(BF16)
            return carry

        row_blocks(seq, MLP_ROWS, enter, 0)
        branch[...] = jnp.zeros_like(branch)
        d_hidden[...] = jnp.zeros_like(d_hidden)

    for k in range(steps):

        @pl.when(step == k)
        def _(k=k):
            for copy in load(k):
                copy.wait()

    @pl.when(step < steps)
    def _():
        bias_here = d_bias[:, at_chunk]

        def forward(rows, carry):
            pre = matmul(hidden[rows, :], w1[...]) + bias_here
            half = 0.5 * (1.0 + lax.erf(pre * 0.7071067811865476))
            slope[rows, at_chunk] = (half + pre * jnp.exp(-0.5 * pre * pre) * 0.3989422804014327).astype(BF16)
            low = (pre * half).astype(BF16)
            act[rows, at_chunk] = low
            branch[rows, :] += matmul(low, w2[...])
            return carry

        row_blocks(seq, MLP_ROWS, forward, 0)

    @pl.when(step == steps)
    def _():
        def finish(rows, total):
            mlp = branch[rows, :] + fc2_bias
            d_mixed[rows, :] = (resid[rows, :] + gain_out * mlp).astype(BF16)
            return total + row_sum(upstream[rows, :] * mlp)

        vector[0, 0:1, :] = row_blocks(seq, MLP_ROWS, finish, jnp.zeros((1, width), F32))
        ordered = t_matmul(to_slot[...], d_mixed[...]).astype(BF16)
        blocks_out[...] = ordered.reshape(blocks_out.shape)
        move.start()

    if direct:
        for k in range(len(grads)):

            @pl.when(step == steps + k)
            def _(k=k):
                at = sum(FC2_SPANS[:k])
                partial = t_matmul(act[...], d_branch[:, at : at + FC2_SPANS[k]]).astype(BF16)
                grads[k][...] = partial.reshape(grads[k].shape)
    else:

        @pl.when(step == steps)
        def _():
            p_fc2[0][...] = t_matmul(act[...], d_branch[...]).astype(BF16)

    run_here(0)

    @pl.when(step >= steps)
    def _():
        def backward(rows, total):
            back = (matmul_t(d_branch[rows, :], w2[...]) * slope[rows, at_chunk].astype(F32)).astype(BF16)
            d_pre[rows, :] = back
            d_hidden[rows, :] += matmul_t(back, w1[...])
            return total + row_sum(back.astype(F32))

        bias_sum = row_blocks(seq, MLP_ROWS, backward, jnp.zeros((1, chunk), F32))
        d_bias[:, at_chunk] = bias_sum
        run_here(2)
        p_fc1[0] = t_matmul(hidden[...], d_pre[...]).astype(BF16)

    @pl.when(step == 2 * steps - 1)
    def _():
        run(3 * steps)

        def leave(rows, totals):
            d_fc2b, d_ln2g, d_ln2b, d_gamma1, d_projb = totals
            d_fc2b += row_sum(d_branch[rows, :].astype(F32))
            normed, factor = normalize(resid[rows, :])
            grad = d_hidden[rows, :]
            d_ln2g += row_sum(grad * normed)
            d_ln2b += row_sum(grad)
            grad = upstream[rows, :] + norm_back(grad, normed, factor, gain2)
            d_resid[rows, :] = grad
            d_gamma1 += row_sum(grad * attn[rows, :])
            grad = (gain1 * grad).astype(BF16)
            d_branch[rows, :] = grad
            d_projb += row_sum(grad.astype(F32))
            d_mixed[rows, :] = matmul_t(grad, w_proj[...]).astype(BF16)
            return d_fc2b, d_ln2g, d_ln2b, d_gamma1, d_projb

        totals = row_blocks(seq, MLP_ROWS, leave, (jnp.zeros((1, width), F32),) * 5)
        run(3 * steps + 1)
        run(3 * steps + 2)
        p_proj[...] = t_matmul(mixed[...], d_branch[...]).astype(BF16)
        zero = jnp.zeros((2, width), F32)
        vector[0, 1:8, :] = jnp.concatenate([*totals, zero], axis=0)
        pieces = [d_bias[:, i * width : (i + 1) * width] for i in range(4)]
        vector[1] = jnp.concatenate(pieces + [zero, zero], axis=0)
        run(3 * steps + 3)
        move.finish()
        output[...] = landed[...]


def fc2_pairs(hidden, half):
    pairs, at = [], 0
    for span in FC2_SPANS:
        part = span // 2
        pairs.append([WeightSum(hidden // 8, at + f * part, part, f == 1, True, half) for f in (0, 1)])
        at += span
    return pairs


def mlp(inputs, mixed, raw_up, to_slot, w_proj, vectors, w1, b1, w2, count, direct):
    seq, width = inputs.shape
    hidden = w1.shape[1]
    chunk = MLP_CHUNK
    steps = hidden // chunk
    pairs = fc2_pairs(hidden, "first") if direct else []
    flat = lambda dtype: jax.ShapeDtypeStruct((seq, width), dtype)
    vmem = lambda dtype: pltpu.VMEM((seq, width), dtype)
    parts = [(2, 2, hidden // 8, span // 2) for span in FC2_SPANS] if direct else [(hidden, width)]
    turn = lambda k: lax.rem(k, steps)
    blocks = (count, seq // count, width)
    return pl.pallas_call(
        functools.partial(mlp_kernel, (count, direct, pairs)),
        grid=(2 * steps,),
        out_shape=[
            jax.ShapeDtypeStruct(blocks, BF16),
            flat(F32),
            flat(BF16),
            jax.ShapeDtypeStruct((width, width), BF16),
            jax.ShapeDtypeStruct((steps, width, chunk), BF16),
            jax.ShapeDtypeStruct((2, 8, width), F32),
        ]
        + [jax.ShapeDtypeStruct(p, BF16) for p in parts],
        in_specs=[
            once(inputs.shape),
            once(mixed.shape),
            once(raw_up.shape),
            once(to_slot.shape),
            once(w_proj.shape),
        ]
        + [whole(v.shape) for v in vectors]
        + [whole(b1.shape), ANY, ANY],
        out_specs=[
            once(blocks),
            once((seq, width)),
            once((seq, width)),
            once((width, width)),
            pl.BlockSpec((1, width, chunk), lambda k: (jnp.maximum(k - steps, 0), 0, 0)),
            whole((2, 8, width)),
        ]
        + [once(p) for p in parts],
        scratch_shapes=[
            vmem(BF16), vmem(BF16), vmem(F32), vmem(F32), vmem(F32), vmem(F32), vmem(F32),
            pltpu.VMEM((seq, hidden), BF16), pltpu.VMEM((seq, hidden), BF16),
            pltpu.VMEM((seq, chunk), BF16), pltpu.VMEM((1, hidden), F32), pltpu.VMEM(blocks, BF16),
            pltpu.VMEM(blocks, BF16),
            pltpu.VMEM((steps, width, chunk), BF16), pltpu.VMEM((steps, chunk, width), BF16),
            pltpu.SemaphoreType.DMA((2 * steps,)),
        ]
        + Exchange(count).scratch()
        + [pltpu.VMEM((2, 2, 2, hidden // 8, span), BF16) for span in FC2_SPANS[: len(pairs)]]
        + [s for pair in pairs for part in pair for s in part.scratch()],
        compiler_params=pltpu.CompilerParams(
            collective_id=1, has_side_effects=True, vmem_limit_bytes=VMEM_LIMIT
        ),
        name="mlp",
    )(inputs, mixed, raw_up, to_slot, w_proj, *vectors, b1, w1, w2)


def swap(value, axis, bit, count):
    return lax.ppermute(value, axis, [(i, i ^ bit) for i in range(count)])


def bits_of(count):
    return [1 << i for i in range(count.bit_length() - 1)]


def scatter_sum(grad, batch, blk):
    places = [("batch", bit, batch) for bit in bits_of(batch)][::-1]
    places += [("blk", bit, blk) for bit in bits_of(blk)][::-1]
    value = grad.reshape((2,) * len(places) + (grad.shape[0] >> len(places), grad.shape[1]))
    left = list(places)
    for spot in places:
        axis, bit, count = spot
        at = left.index(spot)
        left.remove(spot)
        mine = jnp.bitwise_and(lax.axis_index(axis) // bit, 1)
        sent = lax.dynamic_index_in_dim(value, 1 - mine, at, keepdims=False)
        kept = lax.dynamic_index_in_dim(value, mine, at, keepdims=False)
        got = swap(sent, axis, bit, count)
        value = kept.astype(F32) + got.astype(F32)
        if left:
            value = value.astype(BF16)
    return value


def total_sum(value, batch, blk):
    for bit in bits_of(batch):
        value = value + swap(value, "batch", bit, batch)
    for bit in bits_of(blk):
        value = value + swap(value, "blk", bit, blk)
    return value


def unpack_kernel(plan, early, late, table, *refs):
    refs = list(refs)
    take = lambda n: [refs.pop(0) for _ in range(n)]
    sources = [take(n) for n in plan]
    vectors = take(11)
    out_low, out_high = take(2)
    targets = take(len(plan))
    turned = take(1)[0]
    for group, target in zip(sources, targets):
        at = 0
        for source in group:
            size = source.shape[-1]
            target[..., at : at + size] = source[...]
            at += size
    for i in range(6):
        vectors[i][...] = early[0, i : i + 1, :].reshape(vectors[i].shape)
    for n in range(4):
        rows = [late[6 * n + k : 6 * n + k + 1, :] for k in range(6)]
        vectors[6 + n][...] = jnp.concatenate(rows, axis=1).reshape(vectors[6 + n].shape)
    rows = [early[1, i : i + 1, :] for i in range(4)]
    vectors[10][...] = jnp.concatenate(rows, axis=1).reshape(vectors[10].shape)
    heads = out_low.shape[0]
    for n, (out, side, pad) in enumerate(((out_low, SIDE_LOW, G_HIGH - G_LOW), (out_high, SIDE, 0))):
        value = jnp.concatenate([table[n, k * 48 : (k + 1) * 48, :] for k in range(heads // 2)], axis=1)
        turned[n] = jnp.concatenate([value, jnp.zeros((80, 64 * heads), F32)], axis=0).T
        here = turned.at[n]
        for r in range(side):
            rows = pl.ds(SIDE - 1 - r - pad, heads, stride=64)
            out[:, r * side : (r + 1) * side] = here[rows, :][:, pad : pad + side]
        for i in range(3):
            out[:, side * side + i : side * side + i + 1] = here[pl.ds(i, heads, stride=64), :][:, 47:48]


def unpack(early, late, table, groups, width, hidden, heads):
    outs = [jax.ShapeDtypeStruct((width,), F32)] * 10 + [jax.ShapeDtypeStruct((hidden,), F32)]
    outs += [jax.ShapeDtypeStruct((heads, side * side + 3), F32) for side in (SIDE_LOW, SIDE)]
    outs += [
        jax.ShapeDtypeStruct(g[0].shape[:-1] + (sum(p.shape[-1] for p in g),), g[0].dtype) for g in groups
    ]
    pieces = [p for g in groups for p in g]
    vmem = pl.BlockSpec(memory_space=pltpu.VMEM)
    result = pl.pallas_call(
        functools.partial(unpack_kernel, [len(g) for g in groups]),
        out_shape=outs,
        in_specs=[vmem] * (3 + len(pieces)),
        out_specs=[vmem] * (13 + len(groups)),
        scratch_shapes=[pltpu.VMEM((2, 64 * heads, 128), F32)],
        compiler_params=pltpu.CompilerParams(vmem_limit_bytes=VMEM_LIMIT),
        name="unpack",
    )(early, late, table, *pieces)
    return result[:11], result[11].T, result[12].T, result[13:]


def swap(value, axis, bit, count):
    return lax.ppermute(value, axis, [(i, i ^ bit) for i in range(count)])


def bits_of(count):
    return [1 << i for i in range(count.bit_length() - 1)]


def scatter_sum(grad, batch, blk):
    places = [("batch", bit, batch) for bit in bits_of(batch)][::-1]
    places += [("blk", bit, blk) for bit in bits_of(blk)][::-1]
    value = grad.reshape((2,) * len(places) + (grad.shape[0] >> len(places), grad.shape[1]))
    left = list(places)
    for spot in places:
        axis, bit, count = spot
        at = left.index(spot)
        left.remove(spot)
        mine = jnp.bitwise_and(lax.axis_index(axis) // bit, 1)
        sent = lax.dynamic_index_in_dim(value, 1 - mine, at, keepdims=False)
        kept = lax.dynamic_index_in_dim(value, mine, at, keepdims=False)
        got = swap(sent, axis, bit, count)
        value = kept.astype(F32) + got.astype(F32)
        if left:
            value = value.astype(BF16)
    return value


def total_sum(value, batch, blk):
    for bit in bits_of(batch):
        value = value + swap(value, "batch", bit, batch)
    for bit in bits_of(blk):
        value = value + swap(value, "blk", bit, blk)
    return value


def shards(
    batch,
    blk,
    tokens,
    resolution,
    positions,
    ln1_gain,
    ln1_bias,
    w_qkv,
    q_bias,
    v_bias,
    w_proj,
    proj_bias,
    gamma1,
    ln2_gain,
    ln2_bias,
    w_fc1,
    fc1_bias,
    w_fc2,
    fc2_bias,
    gamma2,
    rel_low,
    rel_high,
    grad_out,
):
    images, rows, width = tokens.shape
    seq = positions.shape[1]
    heads = rel_low.shape[1]
    assert images == blk and rows * blk == seq and width == heads * 64
    direct = (batch, blk) == (8, 4)
    bits = jnp.asarray(lane_tables())
    patches = jnp.asarray(slot_tables(seq)[2].T, F32)
    to_slot, inputs, qkv, probs, mixed, raw_up = front(
        resolution,
        positions,
        rel_low,
        rel_high,
        bits,
        patches,
        (ln1_gain, ln1_bias, q_bias, v_bias),
        w_qkv,
        tokens,
        grad_out,
        blk,
    )
    output, d_resid, d_mixed, p_proj, p_fc1, early, *p_fc2 = mlp(
        inputs,
        mixed,
        raw_up.reshape(seq, width),
        to_slot,
        w_proj,
        (proj_bias, gamma1, ln2_gain, ln2_bias, fc2_bias, gamma2),
        w_fc1,
        fc1_bias,
        w_fc2,
        blk,
        direct,
    )
    grad_tokens, g_qkv, *sums, late, d_table = tail(
        resolution,
        qkv,
        probs,
        d_mixed,
        patches,
        bits,
        (ln1_gain, ln1_bias),
        inputs,
        d_resid,
        to_slot,
        w_qkv,
        (p_fc1, p_proj),
        p_fc2,
        early,
        blk,
        direct,
    )
    groups = [[output], [grad_tokens]]
    if direct:
        g_fc1, g_proj, g_fc2, early = sums
        groups += [[g] for g in (g_fc1, g_fc2, g_proj, g_qkv)]
    else:
        g_fc1, g_fc2, g_proj, g_qkv = [scatter_sum(g, batch, blk) for g in (p_fc1.transpose(1, 0, 2).reshape(width, -1), *p_fc2, p_proj, g_qkv)]
        early, late, d_table = [total_sum(v, batch, blk) for v in (early, late, d_table)]
    vectors, s_low, s_high, rest = unpack(early, late, d_table, groups, width, w_fc1.shape[1], heads)
    s_gamma2, s_fc2b, s_ln2g, s_ln2b, s_gamma1, s_projb, s_ln1g, s_ln1b, s_qb, s_vb, s_fc1b = vectors
    output, grad_tokens = rest[:2]
    if direct:
        g_fc1, g_fc2, g_proj, g_qkv = rest[2:]
    return (
        output,
        grad_tokens,
        s_ln1g,
        s_ln1b,
        g_qkv,
        s_qb,
        s_vb,
        g_proj,
        s_projb,
        s_gamma1,
        s_ln2g,
        s_ln2b,
        g_fc1,
        s_fc1b,
        g_fc2,
        s_fc2b,
        s_gamma2,
        s_low,
        s_high,
    )


def solution(mesh):
    rows = P("batch", "blk", None)
    shared = P(("batch", "blk"), None)
    in_specs = (rows, P("batch"), P("batch", None)) + (P(),) * 17 + (rows,)
    out_specs = (
        (rows, rows, P(), P(), shared, P(), P(), shared)
        + (P(),) * 4
        + (shared, P(), shared)
        + (P(),) * 4
    )
    return jax.shard_map(
        functools.partial(shards, mesh.shape["batch"], mesh.shape["blk"]),
        mesh=mesh,
        in_specs=in_specs,
        out_specs=out_specs,
        check_vma=False,
    )
```

profile of v0, /device:TPU:0, one launch (start us, length us, event | category | flops | bytes accessed | tf_op | source)
XLA Modules:
  0.0 198.9 jit_solution(6950661055802342810)
XLA Ops:
  0.7 50.4 %front.1 = (bf16[640,640]{1,0:T(8,128)(2,1)}, f32[640,768]{1,0:T(8,128)}, bf16[640,2304]{1,0:T(8,128)(2,1)}, bf16[12,640,640]{2,1,0:T(8,128)(2,1)}, bf16[640,768...) custom-call(s32[4]{0:T(128)} %refs_0_.1, s32[4,640]{1,0:T(4,128)} %cells.1, bf16[12,732]{1,0:T(8,128)(2,1)} %bitcast.11, ...), custom_call_target="tpu_custom_call" | custom-call | tf_op jit(solution)/shard_map/front/pallas_call | solution.py:210
  51.1 55.9 %mlp.1 = (bf16[4,160,768]{2,1,0:T(8,128)(2,1)}, f32[640,768]{1,0:T(8,128)}, bf16[640,768]{1,0:T(8,128)(2,1)}, bf16[768,768]{1,0:T(8,128)(2,1)}, bf16[6,768,512]{...) custom-call(f32[640,768]{1,0:T(8,128)} %get-tuple-element.62.refs_0_.r, ...), custom_call_target="tpu_custom_call" | custom-call | tf_op jit(solution)/shard_map/mlp/pallas_call | solution.py:1057
  107.0 87.7 %tail.1 = (bf16[4,160,768]{2,1,0:T(8,128)(2,1)}, f32[24,2304]{1,0:T(8,128)}, f32[24,3072]{1,0:T(8,128)}, f32[24,768]{1,0:T(8,128)}, f32[96,768]{1,0:T(8,128)}, /...) custom-call(s32[4]{0:T(128)} %refs_0_.1, ...), custom_call_target="tpu_custom_call" | custom-call | tf_op jit(solution)/shard_map/tail/pallas_call | solution.py:506
  194.7 4.1 %unpack.1 = (f32[768]{0:T(1024)}, f32[768]{0:T(1024)}, f32[768]{0:T(1024)}, f32[768]{0:T(1024)}, f32[768]{0:T(1024)}, /*index=5*/f32[768]{0:T(1024)}, f32[768]{0...) custom-call(f32[2,8,768]{2,1,0:T(8,128)} %get-tuple-element.73.early, ...), custom_call_target="tpu_custom_call" | custom-call | tf_op jit(solution)/shard_map/unpack/pallas_call | solution.py:1181
where the time goes:
time: 199 us
  Pallas kernels  198 us (99%)
    pallas_call x1, Pallas kernels, tail(): pl.pallas_call(functools.partial(tail_kernel, (count, groups, len(views))...  87.7 us
    pallas_call x1, Pallas kernels, mlp(): pl.pallas_call(functools.partial(mlp_kernel, (count, direct, pairs)), gri...  55.9 us
    pallas_call x1, Pallas kernels, front(): pl.pallas_call(functools.partial(front_kernel, count), grid=(heads + head...  50.4 us
    pallas_call x1, Pallas kernels, unpack(): pl.pallas_call(functools.partial(unpack_kernel, [len(g) for g in groups])...  4.06 us

commit v1 on v0

--- a/solution.py
+++ b/solution.py
@@ -286,13 +286,9 @@
     return jnp.concatenate([row[:, i : i + 128] for i in range(0, row.shape[1], 128)], axis=0)
 
 
-FC1_SLOTS = ((0, 2, 6, 10, 13, 20, 26), (0, 3, 8, 11, 13, 20, 26), (1, 3, 9, 12, 14, 20, 26))
-PROJ_SLOTS = ((8, 10, 13, 16, 21, 22, 26),)
-QKV_SLOTS = (
-    (8, 10, 13, 16, 21, 22, 26),
-    (9, 11, 16, 17, 21, 22, 26),
-    (12, 13, 17, 18, 21, 22, 26),
-)
+FC1_SLOTS = ((0, 2, 6, 10, 16, 20, 26), (0, 3, 8, 11, 16, 20, 26), (1, 3, 9, 12, 17, 20, 26))
+PROJ_SLOTS = ((8, 10, 16, 17, 21, 22, 26),)
+QKV_SLOTS = ((8, 10, 16, 17, 21, 22, 26), (9, 11, 16, 17, 21, 22, 26), (12, 13, 17, 18, 21, 22, 26))
 FC2_SLOTS = ((0, 4, 7, 18, 26), (0, 5, 8, 18, 26))
 EARLY_SLOTS = (0, 1, 3, 5, 7, 9)
 TABLE_SLOTS = ((8, 9, 11, 16, 17, 18), (12, 13, 16, 17, 18, 19))

time: 199 us -> 199 us (level)
  no operation moved by 1% of the time
where the time goes in v1:
time: 199 us
  Pallas kernels  198 us (99%)
    pallas_call x1, Pallas kernels, tail(): pl.pallas_call(functools.partial(tail_kernel, (count, groups, len(views))...  88.1 us
    pallas_call x1, Pallas kernels, mlp(): pl.pallas_call(functools.partial(mlp_kernel, (count, direct, pairs)), gri...  55.9 us
    pallas_call x1, Pallas kernels, front(): pl.pallas_call(functools.partial(front_kernel, count), grid=(heads + head...  50.4 us
    pallas_call x1, Pallas kernels, unpack(): pl.pallas_call(functools.partial(unpack_kernel, [len(g) for g in groups])...  4.06 us

profile of v1, /device:TPU:0, one launch (start us, length us, event | category | flops | bytes accessed | tf_op | source)
XLA Modules:
  0.0 199.3 jit_solution(11810334225995709216)
XLA Ops:
  0.7 50.4 %front.1 = (bf16[640,640]{1,0:T(8,128)(2,1)}, f32[640,768]{1,0:T(8,128)}, bf16[640,2304]{1,0:T(8,128)(2,1)}, bf16[12,640,640]{2,1,0:T(8,128)(2,1)}, bf16[640,768...) custom-call(s32[4]{0:T(128)} %refs_0_.1, s32[4,640]{1,0:T(4,128)} %cells.1, bf16[12,732]{1,0:T(8,128)(2,1)} %bitcast.11, ...), custom_call_target="tpu_custom_call" | custom-call | tf_op jit(solution)/shard_map/front/pallas_call | solution.py:210
  51.1 55.9 %mlp.1 = (bf16[4,160,768]{2,1,0:T(8,128)(2,1)}, f32[640,768]{1,0:T(8,128)}, bf16[640,768]{1,0:T(8,128)(2,1)}, bf16[768,768]{1,0:T(8,128)(2,1)}, bf16[6,768,512]{...) custom-call(f32[640,768]{1,0:T(8,128)} %get-tuple-element.62.refs_0_.r, ...), custom_call_target="tpu_custom_call" | custom-call | tf_op jit(solution)/shard_map/mlp/pallas_call | solution.py:1053
  107.0 88.1 %tail.1 = (bf16[4,160,768]{2,1,0:T(8,128)(2,1)}, f32[24,2304]{1,0:T(8,128)}, f32[24,3072]{1,0:T(8,128)}, f32[24,768]{1,0:T(8,128)}, f32[96,768]{1,0:T(8,128)}, /...) custom-call(s32[4]{0:T(128)} %refs_0_.1, ...), custom_call_target="tpu_custom_call" | custom-call | tf_op jit(solution)/shard_map/tail/pallas_call | solution.py:502
  195.1 4.1 %unpack.1 = (f32[768]{0:T(1024)}, f32[768]{0:T(1024)}, f32[768]{0:T(1024)}, f32[768]{0:T(1024)}, f32[768]{0:T(1024)}, /*index=5*/f32[768]{0:T(1024)}, f32[768]{0...) custom-call(f32[2,8,768]{2,1,0:T(8,128)} %get-tuple-element.73.early, ...), custom_call_target="tpu_custom_call" | custom-call | tf_op jit(solution)/shard_map/unpack/pallas_call | solution.py:1177
